TPU v7x, 256 devices: a whole 4x4x8 slice. The times are simulated.
256 devices in a mesh: acq: 4 (over x), tile: 64 (over z, y, core).
Axes of the slice: x: 4, y: 4, z: 8, core: 2. Of those that a mesh axis runs over, the one named last changes fastest.
Arguments:
- slc: bfloat16 [16, 2, 8192, 1280], P('acq', None, 'tile')
- match: int32 [2, 16], replicated, may hold values from 0 to 3, as said below
- dest: int32 [64, 16, 32, 1], P('tile', 'acq'), may hold values from 0 to 3; in each aligned block of 128 rows (0 to 127, 128 to 255, ..., all dimensions but the last counted through in order) at most 64 rows name the same one
- coherent: int32 [64, 16, 32], P('tile', 'acq'), may hold values 0 or 1
Outputs:
- received: bfloat16 [64, 1024, 2, 128], P('tile', 'acq')
Inputs may be any that keep to these rules, and one draw needn't show every extreme that they name: `match`: within each round, the entries of each aligned run of 4 acquisitions are a permutation of 0 to 3. `dest`: among the 128 rows of one device, at most 64 name the same owner.
All inputs are finite; a program needn't handle non-finite values. No bound on the sum of `coherent` on one device may be relied on, other than what follows from the above.
Results may differ from a plain program's by a relative error of at most 0.001.
Values may be sent and summed in bfloat16 or wider, within the bound.
No kernel may reach another device: no remote copies, remote signals or barrier semaphores. Data moves between devices by JAX's collectives and lax.ppermute only.
A program may use at most 128 MiB of HBM per device.

v0:
```python
import jax
import jax.numpy as jnp
from jax import lax
from jax.sharding import PartitionSpec as P

PATCH = 32
LOOK_L = 4
LOOK_S = 20
BLOCK_ROWS = 4
ROUNDS = 2
power_floor = 0.25
energy_eps = 1e-06


def swapped(x, axis, stride):
    return lax.ppermute(x, axis, [(i, i ^ 1 << stride) for i in range(lax.axis_size(axis))])


def dft_tables():
    counter = jnp.arange(PATCH)
    phase = counter[:, None] * counter[None, :] % PATCH
    angle = phase.astype(jnp.float32) * (2.0 * 3.141592653589793 / PATCH)
    return (jnp.cos(angle), jnp.sin(angle))


def along_axes(real_part, imag_part, cosine, sine_tab, sign, form):
    hold = lax.Precision.HIGHEST
    c_real = jnp.einsum(form, cosine, real_part, precision=hold)
    c_imag = jnp.einsum(form, cosine, imag_part, precision=hold)
    s_real = jnp.einsum(form, sine_tab, real_part, precision=hold)
    s_imag = jnp.einsum(form, sine_tab, imag_part, precision=hold)
    return (c_real - sign * s_imag, c_imag + sign * s_real)


def transform(real_part, imag_part, cosine, sine_tab, sign):
    real_part, imag_part = along_axes(
        real_part, imag_part, cosine, sine_tab, sign, "jk,aPkQl->aPjQl"
    )
    return along_axes(real_part, imag_part, cosine, sine_tab, sign, "lm,aPkQm->aPkQl")


def cross_looks(left, right, picks):
    acq_dev, _, line_count, sample_count = left.shape
    other = jnp.take(right, picks, axis=0)
    own_real = left[:, 0].astype(jnp.float32)
    own_imag = left[:, 1].astype(jnp.float32)
    other_real = other[:, 0].astype(jnp.float32)
    other_imag = other[:, 1].astype(jnp.float32)
    real_part = own_real * other_real + own_imag * other_imag
    imag_part = own_imag * other_real - own_real * other_imag
    stacked = jnp.stack([real_part, imag_part], axis=1)
    stacked = stacked.reshape(
        acq_dev, 2, line_count // LOOK_L, LOOK_L, sample_count // LOOK_S, LOOK_S
    )
    return jnp.sum(stacked, axis=(3, 5)) / (LOOK_L * LOOK_S)


def shards(slc, match, dest, coherent):
    acq_dev, _, lines_dev, samples_dev = slc.shape
    n_acq = lax.axis_size("acq")
    n_tile = lax.axis_size("tile")
    far_bit = n_acq.bit_length() - 2
    grid_count = lines_dev * n_tile // LOOK_L * (samples_dev // LOOK_S)
    patch_rows = lines_dev // LOOK_L // PATCH
    patch_cols = samples_dev // LOOK_S // PATCH
    cosine, sine_tab = dft_tables()
    my_group = lax.axis_index("acq")

    def swap_tiles(tiles, round_number):
        if round_number == 0:
            return swapped(tiles, "acq", 0)
        return swapped(tiles, "acq", far_bit)

    order_list = [0, 1]
    looked_all = {}
    filtered_all = {}
    for round_number in order_list:
        own_match = lax.dynamic_slice_in_dim(match[round_number], my_group * acq_dev, acq_dev)
        group_tiles = swap_tiles(slc, round_number)
        looked_all[round_number] = cross_looks(slc, group_tiles, own_match)
        local_looked = looked_all[round_number]
        total = lax.psum(
            jnp.sum(local_looked[:, 0] ** 2 + local_looked[:, 1] ** 2, axis=(1, 2)), "tile"
        )
        energy = total / grid_count + energy_eps
        looked = looked_all[round_number]
        shape_six = (acq_dev, patch_rows, PATCH, patch_cols, PATCH)
        real_part = looked[:, 0].reshape(shape_six)
        imag_part = looked[:, 1].reshape(shape_six)
        spec_real, spec_imag = transform(real_part, imag_part, cosine, sine_tab, -1.0)
        scale = energy[:, None, None, None, None]
        power = (spec_real**2 + spec_imag**2) / (PATCH * PATCH * scale)
        weight = (power + power_floor) ** 0.25
        back_real, back_imag = transform(
            weight * spec_real, weight * spec_imag, cosine, sine_tab, 1.0
        )
        norm_factor = 1.0 / (PATCH * PATCH * jnp.sqrt(scale))
        parts = jnp.stack([back_real * norm_factor, back_imag * norm_factor], axis=-1)
        parts = parts.reshape(
            acq_dev, patch_rows, PATCH // BLOCK_ROWS, BLOCK_ROWS, patch_cols, PATCH, 2
        )
        parts = jnp.transpose(parts, (0, 1, 2, 4, 6, 3, 5))
        filtered_all[round_number] = parts.reshape(
            acq_dev, patch_rows * (PATCH // BLOCK_ROWS) * patch_cols, 2, BLOCK_ROWS * PATCH
        )
    stacked = jnp.stack([filtered_all[round_number] for round_number in range(ROUNDS)], axis=1)
    block_len = BLOCK_ROWS * PATCH
    rows_dev = stacked.shape[0] * stacked.shape[1] * stacked.shape[2]
    cap_rows = max(3, 2 * ((rows_dev + n_acq - 1) // n_acq))
    stacked = stacked.reshape(rows_dev, 2, block_len)
    mask_rows = coherent.reshape(rows_dev).astype(jnp.float32)
    value = (stacked * mask_rows[:, None, None]).astype(jnp.bfloat16)
    owner = dest.reshape(rows_dev)
    onehot = (owner[:, None] == jnp.arange(n_acq)).astype(jnp.int32)
    rank = jnp.sum((jnp.cumsum(onehot, axis=0) - onehot) * onehot, axis=1)
    hits = (onehot[:, :, None] == 1) & (rank[:, None, None] == jnp.arange(cap_rows)[None, None, :])
    select = hits.astype(jnp.bfloat16).reshape(rows_dev, n_acq * cap_rows)
    outgoing = jnp.einsum("ks,kcp->scp", select, value, preferred_element_type=jnp.float32).astype(
        jnp.bfloat16
    )
    incoming = lax.all_to_all(outgoing, "acq", split_axis=0, concat_axis=0, tiled=True)
    return incoming[None]


def solution(mesh):
    return jax.shard_map(
        shards,
        mesh=mesh,
        in_specs=(
            P("acq", None, "tile", None),
            P(),
            P("tile", "acq", None, None),
            P("tile", "acq", None),
        ),
        out_specs=P("tile", "acq", None, None),
        check_vma=False,
    )
```

profile of v0, /device:TPU:2, one launch (start us, length us, event | category | flops | bytes accessed | tf_op | source)
XLA Modules:
  0.0 392.0 jit_solution(11845834372850043596)
XLA Ops:
  0.0 2.1 collective-permute-start.1
  2.1 1.4 collective-permute-start
  3.6 0.7 convert_element_type.142
  4.3 0.5 broadcast.327
  4.8 1.3 reduce.5
  6.4 0.2 reduce_window_sum.11
  6.6 0.8 fusion.240
  7.6 0.2 select_reduce_fusion
  7.8 53.8 %collective-permute-done.1 = bf16[4,2,128,1280]{3,2,1,0:T(8,128)(2,1)} collective-permute-done((bf16[4,2,128,1280]{3,2,1,0:T(8,128)(2,1)}, bf16[4,2,128,1280]{3,2,1,0:T(8,128)(2,1)}, u32[]{:S(2)}, u32[]{:S(2)}) %collective-permute-start.1) | collective-permute-done | bytes 2621472 | tf_op jit(solution)/shard_map/ppermute | solution.py:16
  61.6 2.5 gather_fusion.1
  64.0 1.8 broadcast_select_fusion
  65.9 50.8 %collective-permute-done = bf16[4,2,128,1280]{3,2,1,0:T(8,128)(2,1)} collective-permute-done((bf16[4,2,128,1280]{3,2,1,0:T(8,128)(2,1)}, bf16[4,2,128,1280]{3,2,1,0:T(8,128)(2,1)}, u32[]{:S(2)}, u32[]{:S(2)}) %collective-permute-start) | collective-permute-done | bytes 2621472 | tf_op jit(solution)/shard_map/ppermute | solution.py:16
  116.6 2.5 gather_fusion
  119.1 0.3 broadcast_select_fusion.1
  119.4 1.4 copy-done
  120.8 0.8 copy-done.1
  121.6 4.0 %fusion = (f32[4,1,128,1280]{3,2,1,0:T(8,128)}, f32[4,1,128,1280]{3,2,1,0:T(8,128)}, f32[4,1,128,1280]{3,2,1,0:T(8,128)S(1)}, f32[4,1,128,1280]{3,2,1,0:T(8,128)}) fusion(bf16[4,2,128,1280]{3,2,1,0:T(8,128)(2,1)S(1)} %broadcast_select_fusion.1, bf16[4,2,128,1280]{3,2,1,0:T(8,128)(2,1)S(1)} %copy-done.1, bf16[4,2,128,1280]{3,2,1,0:T(8,128)(2,1)S(1)} %copy-done), kind=kLoop, calls=%fused_computation.12 | loop fusion | flops 11796480 | bytes 18350080 | tf_op jit(solution)/shard_map/add | solution.py:49
  125.6 21.7 %stack.39 = f32[4,1,32,4,64,20]{5,4,3,2,0,1:T(8,128)} reshape(f32[4,1,128,1280]{3,2,1,0:T(8,128)} %get-tuple-element.12) | data formatting | bytes 5242880 | tf_op jit(solution)/shard_map/stack | solution.py:51
  147.3 21.7 %stack.40 = f32[4,1,32,4,64,20]{5,4,3,2,0,1:T(8,128)} reshape(f32[4,1,128,1280]{3,2,1,0:T(8,128)} %get-tuple-element.13) | data formatting | bytes 5242880 | tf_op jit(solution)/shard_map/stack | solution.py:51
  168.9 12.7 %maximum_reduce_fusion = f32[4,2,32,64]{3,2,0,1:T(8,128)S(1)} fusion(f32[4,1,32,4,64,20]{5,4,3,2,0,1:T(8,128)} %stack.40, f32[4,1,32,4,64,20]{5,4,3,2,0,1:T(8,128)} %stack.39), kind=kLoop, calls=%fused_computation.2 | loop fusion | flops 2605056 | bytes 5308416 | tf_op jit(solution)/shard_map/reduce_sum | solution.py:55
  181.7 0.1 fusion.239
  181.9 0.3 convolution_multiply_fusion.6
  182.4 0.3 convolution_multiply_fusion.7
  182.7 0.3 fusion.10
  183.1 0.4 convolution_multiply_fusion.5
  183.5 0.3 fusion.11
  183.8 0.4 convolution_multiply_fusion.4
  184.2 0.4 convolution_subtract_fusion.6
  184.6 0.4 convolution_add_fusion.6
  185.0 21.7 %stack.45 = f32[4,1,32,4,64,20]{5,4,3,2,0,1:T(8,128)} reshape(f32[4,1,128,1280]{3,2,1,0:T(8,128)} %get-tuple-element.17) | data formatting | bytes 5242880 | tf_op jit(solution)/shard_map/stack | solution.py:51
  206.7 20.9 %stack.46 = f32[4,1,32,4,64,20]{5,4,3,2,0,1:T(8,128)} reshape(f32[4,1,128,1280]{3,2,1,0:T(8,128)S(1)} %get-tuple-element.16) | data formatting | bytes 5242880 | tf_op jit(solution)/shard_map/stack | solution.py:51
  227.6 12.7 %maximum_reduce_fusion.1 = f32[4,2,32,64]{3,2,0,1:T(8,128)S(1)} fusion(f32[4,1,32,4,64,20]{5,4,3,2,0,1:T(8,128)} %stack.46, f32[4,1,32,4,64,20]{5,4,3,2,0,1:T(8,128)} %stack.45), kind=kLoop, calls=%fused_computation.3 | loop fusion | flops 2605056 | bytes 5308416 | tf_op jit(solution)/shard_map/reduce_sum | solution.py:55
  240.4 0.1 add_reduce_fusion
  240.5 131.1 %all-reduce = (f32[4]{0:T(128)S(1)}, f32[4]{0:T(128)S(1)}) all-reduce(f32[4]{0:T(128)S(1)} %get-tuple-element.21, f32[4]{0:T(128)S(1)} %get-tuple-element.19), channel_id=1, replica_groups=mesh['acq'=4,'tile'=64] {'tile'}, use_global_device_ids=true, to_apply=%region_7.9 | all-reduce | flops 8 | bytes 64 | tf_op jit(solution)/shard_map/psum | solution.py:82
  371.6 0.5 fusion.60
  372.1 0.5 fusion.56
  372.7 0.3 convolution_multiply_fusion.2
  373.2 0.3 convolution_multiply_fusion.3
  373.5 0.3 fusion.6
  373.9 0.4 convolution_multiply_fusion.1
  374.3 0.3 fusion.7
  374.6 0.4 convolution_multiply_fusion
  375.0 0.4 convolution_subtract_fusion.2
  375.4 0.4 convolution_add_fusion.2
  375.8 0.5 fusion.48
  376.3 0.5 fusion.44
  376.9 0.5 fusion.9
  377.4 0.4 fusion.58
  377.8 0.5 fusion.8
  378.3 0.4 fusion.54
  378.7 0.4 fusion.12
  379.1 0.4 fusion.13
  379.6 0.2 stack_reshape.6
  379.8 0.5 fusion.5
  380.3 0.4 fusion.46
  380.7 0.5 fusion.4
  381.2 0.4 fusion.42
  381.6 0.4 fusion.14
  382.0 0.4 fusion.15
  382.5 0.2 stack_reshape.7
  382.8 0.2 convolution_convert_fusion
  383.0 0.1 copy.171
  383.1 8.2 %all_to_all.5 = bf16[256,2,128]{2,1,0:T(2,128)(2,1)S(1)} all-to-all(bf16[256,2,128]{2,1,0:T(2,128)(2,1)S(1)} %copy.171), channel_id=1, replica_groups=mesh['acq'=4,'tile'=64] {'acq'}, dimensions={0} | all-to-all | bytes 262144 | tf_op jit(solution)/shard_map/all_to_all | solution.py:121
  391.3 0.7 copy.205
  (24 shorter events, 1.2 us)
Async XLA Ops:
  0.0 61.6 %collective-permute-start.1 = (bf16[4,2,128,1280]{3,2,1,0:T(8,128)(2,1)}, bf16[4,2,128,1280]{3,2,1,0:T(8,128)(2,1)}, u32[]{:S(2)}, u32[]{:S(2)}) collective-permute-start(bf16[4,2,128,1280]{3,2,1,0:T(8,128)(2,1)} %param.6), channel_id=1, source_target_pairs={{0,128},{64,192},{128,0},{192,64},{1,129},{65,193},{129,1},{193,65... | collective-permute-start | bytes 7864328 | tf_op jit(solution)/shard_map/ppermute | solution.py:16
  2.1 114.5 %collective-permute-start = (bf16[4,2,128,1280]{3,2,1,0:T(8,128)(2,1)}, bf16[4,2,128,1280]{3,2,1,0:T(8,128)(2,1)}, u32[]{:S(2)}, u32[]{:S(2)}) collective-permute-start(bf16[4,2,128,1280]{3,2,1,0:T(8,128)(2,1)} %param.6), channel_id=1, source_target_pairs={{0,64},{64,0},{128,192},{192,128},{1,65},{65,1},{129,193},{193,129... | collective-permute-start | bytes 7864328 | tf_op jit(solution)/shard_map/ppermute | solution.py:16
  119.1 1.7 copy-start
  119.1 2.5 copy-start.1
where the time goes:
time: 392 us
  blocking collectives  139 us (35%)
  waiting for transfers between devices  105 us (27%)
  local copies, waits for them, and re-layouts  96 us (24%)
  other arithmetic  34.8 us (9%)
  matrix products  13.3 us (3%)
    psum x1, blocking collectives, shards(): lax.psum(jnp.sum(local_looked[:, 0] ** 2 + local_looked[:, 1] ** 2, axis=...  131 us
    ppermute x2, waiting for transfers between devices, swapped(): lax.ppermute(x, axis, [(i, i ^ 1 << stride) for i in range(lax.axis_size(...  105 us
    another operation x4, local copies, waits for them, and re-layouts, cross_looks(): stacked = jnp.stack([real_part, imag_part], axis=1)  85.9 us
    reduce_sum x2, other arithmetic, cross_looks(): return jnp.sum(stacked, axis=(3, 5)) / (LOOK_L * LOOK_S)  25.5 us
    all_to_all x1, blocking collectives, shards(): lax.all_to_all(outgoing, 'acq', split_axis=0, concat_axis=0, tiled=True)  8.18 us
  transfers between devices with their start and end apart: 2, of which 2 were waited for; matrix products, arithmetic and copies ran while one was open for 2% of the time, Pallas kernels for 0%

commit v1 on v0

--- a/solution.py
+++ b/solution.py
@@ -79,8 +79,12 @@
         group_tiles = swap_tiles(slc, round_number)
         looked_all[round_number] = cross_looks(slc, group_tiles, own_match)
         local_looked = looked_all[round_number]
-        total = lax.psum(
-            jnp.sum(local_looked[:, 0] ** 2 + local_looked[:, 1] ** 2, axis=(1, 2)), "tile"
+
+        def expand_loads(point):
+            return lax.all_gather(point, axis_name="tile").sum(axis=0)
+
+        total = expand_loads(
+            jnp.sum(local_looked[:, 0] ** 2 + local_looked[:, 1] ** 2, axis=(1, 2))
         )
         energy = total / grid_count + energy_eps
         looked = looked_all[round_number]

time: 392 us -> 393 us (level)
    psum x1 -> x0, blocking collectives: 131 us -> none  [shards(): lax.psum(jnp.sum(local_looked[:, 0] ** 2 + local_looked[:, 1] ** 2, axis=...]
    unnamed x0 -> x1, blocking collectives: none -> 131 us
where the time goes in v1:
time: 393 us
  blocking collectives  139 us (35%)
  waiting for transfers between devices  103 us (26%)
  local copies, waits for them, and re-layouts  97.9 us (25%)
  other arithmetic  34.9 us (9%)
  matrix products  13.3 us (3%)
    unnamed x1, blocking collectives  131 us
    ppermute x2, waiting for transfers between devices, swapped(): lax.ppermute(x, axis, [(i, i ^ 1 << stride) for i in range(lax.axis_size(...  103 us
    another operation x4, local copies, waits for them, and re-layouts, cross_looks(): stacked = jnp.stack([real_part, imag_part], axis=1)  85.9 us
    reduce_sum x2, other arithmetic, cross_looks(): return jnp.sum(stacked, axis=(3, 5)) / (LOOK_L * LOOK_S)  25.5 us
    all_to_all x1, blocking collectives, shards(): lax.all_to_all(outgoing, 'acq', split_axis=0, concat_axis=0, tiled=True)  8.19 us
  transfers between devices with their start and end apart: 2, of which 2 were waited for; matrix products, arithmetic and copies ran while one was open for 2% of the time, Pallas kernels for 0%

profile of v1, /device:TPU:2, one launch (start us, length us, event | category | flops | bytes accessed | tf_op | source)
XLA Modules:
  0.0 392.5 jit_solution(3377520415127960505)
XLA Ops:
  0.0 2.1 collective-permute-start.1
  2.1 1.4 collective-permute-start
  3.6 0.7 convert_element_type.142
  4.3 0.5 broadcast.377
  4.8 1.3 reduce.5
  6.4 0.2 reduce_window_sum.11
  6.6 1.3 dynamic-slice.2
  8.6 0.8 fusion.240
  9.5 0.2 select_reduce_fusion
  9.7 51.9 %collective-permute-done.1 = bf16[4,2,128,1280]{3,2,1,0:T(8,128)(2,1)} collective-permute-done((bf16[4,2,128,1280]{3,2,1,0:T(8,128)(2,1)}, bf16[4,2,128,1280]{3,2,1,0:T(8,128)(2,1)}, u32[]{:S(2)}, u32[]{:S(2)}) %collective-permute-start.1) | collective-permute-done | bytes 2621472 | tf_op jit(solution)/shard_map/ppermute | solution.py:16
  61.6 2.5 gather_fusion.1
  64.0 1.8 broadcast_select_fusion
  65.9 50.8 %collective-permute-done = bf16[4,2,128,1280]{3,2,1,0:T(8,128)(2,1)} collective-permute-done((bf16[4,2,128,1280]{3,2,1,0:T(8,128)(2,1)}, bf16[4,2,128,1280]{3,2,1,0:T(8,128)(2,1)}, u32[]{:S(2)}, u32[]{:S(2)}) %collective-permute-start) | collective-permute-done | bytes 2621472 | tf_op jit(solution)/shard_map/ppermute | solution.py:16
  116.6 2.5 gather_fusion
  119.1 0.3 broadcast_select_fusion.1
  119.4 1.4 copy-done
  120.8 0.8 copy-done.1
  121.6 4.0 %fusion = (f32[4,1,128,1280]{3,2,1,0:T(8,128)}, f32[4,1,128,1280]{3,2,1,0:T(8,128)}, f32[4,1,128,1280]{3,2,1,0:T(8,128)S(1)}, f32[4,1,128,1280]{3,2,1,0:T(8,128)}) fusion(bf16[4,2,128,1280]{3,2,1,0:T(8,128)(2,1)S(1)} %broadcast_select_fusion.1, bf16[4,2,128,1280]{3,2,1,0:T(8,128)(2,1)S(1)} %copy-done.1, bf16[4,2,128,1280]{3,2,1,0:T(8,128)(2,1)S(1)} %copy-done), kind=kLoop, calls=%fused_computation.12 | loop fusion | flops 11796480 | bytes 18350080 | tf_op jit(solution)/shard_map/add | solution.py:49
  125.6 21.7 %stack.39 = f32[4,1,32,4,64,20]{5,4,3,2,0,1:T(8,128)} reshape(f32[4,1,128,1280]{3,2,1,0:T(8,128)} %get-tuple-element.12) | data formatting | bytes 5242880 | tf_op jit(solution)/shard_map/stack | solution.py:51
  147.3 21.7 %stack.40 = f32[4,1,32,4,64,20]{5,4,3,2,0,1:T(8,128)} reshape(f32[4,1,128,1280]{3,2,1,0:T(8,128)} %get-tuple-element.13) | data formatting | bytes 5242880 | tf_op jit(solution)/shard_map/stack | solution.py:51
  168.9 12.7 %maximum_reduce_fusion = f32[4,2,32,64]{3,2,0,1:T(8,128)S(1)} fusion(f32[4,1,32,4,64,20]{5,4,3,2,0,1:T(8,128)} %stack.40, f32[4,1,32,4,64,20]{5,4,3,2,0,1:T(8,128)} %stack.39), kind=kLoop, calls=%fused_computation.2 | loop fusion | flops 2605056 | bytes 5308416 | tf_op jit(solution)/shard_map/reduce_sum | solution.py:55
  181.9 0.3 convolution_multiply_fusion.6
  182.4 0.3 convolution_multiply_fusion.7
  182.7 0.3 fusion.10
  183.1 0.4 convolution_multiply_fusion.5
  183.5 0.3 fusion.11
  183.8 0.4 convolution_multiply_fusion.4
  184.2 0.4 convolution_subtract_fusion.6
  184.6 0.4 convolution_add_fusion.6
  185.0 21.7 %stack.45 = f32[4,1,32,4,64,20]{5,4,3,2,0,1:T(8,128)} reshape(f32[4,1,128,1280]{3,2,1,0:T(8,128)} %get-tuple-element.17) | data formatting | bytes 5242880 | tf_op jit(solution)/shard_map/stack | solution.py:51
  206.7 20.9 %stack.46 = f32[4,1,32,4,64,20]{5,4,3,2,0,1:T(8,128)} reshape(f32[4,1,128,1280]{3,2,1,0:T(8,128)S(1)} %get-tuple-element.16) | data formatting | bytes 5242880 | tf_op jit(solution)/shard_map/stack | solution.py:51
  227.6 12.7 %maximum_reduce_fusion.1 = f32[4,2,32,64]{3,2,0,1:T(8,128)S(1)} fusion(f32[4,1,32,4,64,20]{5,4,3,2,0,1:T(8,128)} %stack.46, f32[4,1,32,4,64,20]{5,4,3,2,0,1:T(8,128)} %stack.45), kind=kLoop, calls=%fused_computation.3 | loop fusion | flops 2605056 | bytes 5308416 | tf_op jit(solution)/shard_map/reduce_sum | solution.py:55
  240.5 0.2 dynamic-update-slice
  240.7 0.2 dynamic-update-slice.1
  240.9 130.9 %all-reduce.2 = (f32[256]{0:T(256)S(1)}, f32[256]{0:T(256)S(1)}) all-reduce(f32[256]{0:T(256)S(1)} %dynamic-update-slice.1, f32[256]{0:T(256)S(1)} %dynamic-update-slice), channel_id=3, replica_groups=mesh['acq'=4,'tile'=64] {'tile'}, use_global_device_ids=true, to_apply=%add.1 | all-reduce | flops 512 | bytes 4096
  372.0 0.5 fusion.60
  372.5 0.5 fusion.56
  373.3 0.3 convolution_multiply_fusion.2
  373.7 0.3 convolution_multiply_fusion.3
  374.1 0.3 fusion.6
  374.4 0.4 convolution_multiply_fusion.1
  374.8 0.3 fusion.7
  375.2 0.4 convolution_multiply_fusion
  375.6 0.4 convolution_subtract_fusion.2
  376.0 0.4 convolution_add_fusion.2
  376.4 0.5 fusion.48
  376.9 0.5 fusion.44
  377.4 0.5 fusion.9
  377.9 0.4 fusion.58
  378.3 0.5 fusion.8
  378.9 0.4 fusion.54
  379.3 0.4 fusion.12
  379.7 0.4 fusion.13
  380.2 0.2 stack_reshape.6
  380.3 0.5 fusion.5
  380.9 0.4 fusion.46
  381.3 0.5 fusion.4
  381.8 0.4 fusion.42
  382.2 0.4 fusion.14
  382.6 0.4 fusion.15
  383.1 0.2 stack_reshape.7
  383.4 0.2 convolution_convert_fusion
  383.7 8.2 %all_to_all.5 = bf16[256,2,128]{2,1,0:T(2,128)(2,1)S(1)} all-to-all(bf16[256,2,128]{2,1,0:T(2,128)(2,1)S(1)} %copy.171), channel_id=1, replica_groups=mesh['acq'=4,'tile'=64] {'acq'}, dimensions={0} | all-to-all | bytes 262144 | tf_op jit(solution)/shard_map/all_to_all | solution.py:125
  391.9 0.7 copy.209
  (34 shorter events, 1.9 us)
Async XLA Ops:
  0.0 61.6 %collective-permute-start.1 = (bf16[4,2,128,1280]{3,2,1,0:T(8,128)(2,1)}, bf16[4,2,128,1280]{3,2,1,0:T(8,128)(2,1)}, u32[]{:S(2)}, u32[]{:S(2)}) collective-permute-start(bf16[4,2,128,1280]{3,2,1,0:T(8,128)(2,1)} %param.6), channel_id=1, source_target_pairs={{0,128},{64,192},{128,0},{192,64},{1,129},{65,193},{129,1},{193,65... | collective-permute-start | bytes 7864328 | tf_op jit(solution)/shard_map/ppermute | solution.py:16
  2.1 114.5 %collective-permute-start = (bf16[4,2,128,1280]{3,2,1,0:T(8,128)(2,1)}, bf16[4,2,128,1280]{3,2,1,0:T(8,128)(2,1)}, u32[]{:S(2)}, u32[]{:S(2)}) collective-permute-start(bf16[4,2,128,1280]{3,2,1,0:T(8,128)(2,1)} %param.6), channel_id=1, source_target_pairs={{0,64},{64,0},{128,192},{192,128},{1,65},{65,1},{129,193},{193,129... | collective-permute-start | bytes 7864328 | tf_op jit(solution)/shard_map/ppermute | solution.py:16
  119.1 1.7 copy-start
  119.1 2.5 copy-start.1
